TPU v7x, 512 devices: a whole 4x8x8 slice. The times are simulated.
512 devices in a mesh: ctx: 128 (over y, z, core), ch: 4 (over x).
Axes of the slice: x: 4, y: 8, z: 8, core: 2. Of those that a mesh axis runs over, the one named last changes fastest.
Arguments:
- query_act: bfloat16 [16384, 4096], P('ctx', 'ch'), may hold values from -6 to 6
- key_act: bfloat16 [16384, 4096], P('ctx', 'ch'), may hold values from -6 to 6
- value_act: bfloat16 [16384, 4096], P('ctx', 'ch'), may hold values from -6 to 6
- short_filter: float32 [128, 4096], P(None, 'ch'), may hold values from -0.5 to 0.5
- long_filter: float32 [16384, 4096], P('ctx', 'ch'), may hold values from -2 to 2
- out_weight: bfloat16 [4096, 4096], P('ch', 'ctx'), may hold values from -0.09375 to 0.09375
Outputs:
- mixed: bfloat16 [16384, 4096], P('ctx', 'ch')
All inputs are finite; a program needn't handle non-finite values.
Results may differ from a plain program's by a relative error of at most 0.02.
Values may be sent and summed in bfloat16 or wider, within the bound.
A program may use at most 128 MiB of HBM per device.

v0:
```python
import math

import jax
import jax.numpy as jnp
import numpy as np
from jax import lax
from jax.experimental import pallas as pl
from jax.experimental.pallas import tpu as pltpu
from jax.sharding import PartitionSpec as P

NX, NY, NZ = 4, 8, 8
CHIPS = NY * NZ
TOK = 128
WIDTH = 1024
OWN = 8
MESH = pl.DeviceIdType.MESH
F32, BF16 = jnp.float32, jnp.bfloat16


def split_table(table):
    high = table.astype(jnp.bfloat16)
    low = (table - high.astype(np.float64)).astype(jnp.bfloat16)
    return high, low


def make_tables():
    blocks = 2 * CHIPS
    half_odd = np.arange(blocks) + 0.5
    index = np.arange(blocks)
    angle = 2 * math.pi * half_odd[:, None] * index[None, :] / (2 * blocks)
    first = np.concatenate([np.cos(angle), -np.sin(angle)], 0)
    fold = split_table(first)
    first_cat = np.concatenate(fold, 1)
    last = split_table(first.T * (2.0 / (2 * blocks * TOK)))
    inner = 2 * math.pi * (np.arange(TOK)[:, None] * np.arange(TOK)[None, :] % TOK) / TOK
    cosine, minus_sine = np.cos(inner), -np.sin(inner)
    second = np.block([[cosine, minus_sine], [-minus_sine, cosine]])
    second_split = split_table(second)
    third_split = split_table(second.T)
    turn = 2 * math.pi * half_odd[:, None] * np.arange(TOK)[None, :] / (2 * blocks * TOK)
    return (
        first_cat,
        np.stack(last),
        np.stack(second_split),
        np.stack(third_split),
        np.stack([np.cos(turn), -np.sin(turn)]).astype(np.float32),
    )


def dot(a, b):
    return jnp.dot(a, b, preferred_element_type=F32)


def halves(value):
    high = value.astype(BF16)
    return high, (value - high.astype(F32)).astype(BF16)


def kernel(
    q_ref, k_ref, v_ref, sf_ref, lf_ref, wt_ref,
    first_ref, last_ref, second_ref, third_ref, turn_ref,
    out_ref,
    tf, tp, tq, ys, taps_t,
    exf_out, exf_in, exp_out, exp_in, exr_out, exr_in,
    send_f, recv_f, send_pq, recv_pq, send_r, recv_r,
    toep, spectrum, wall, hidden,
    hop_out, hop_in, right_out, left_out, from_left, from_right, part_r, part_l,
    ex_send, ex_recv, a_send, a_recv, w1_send, w1_recv, w2_send, w2_recv, wp_send, wp_recv,
    x_send, x_recv,
):
    me = lax.axis_index("ctx")
    x = lax.axis_index("ch")
    m, s = me // 2, me % 2
    o = 1 - s
    y, z = m // NZ, m % NZ
    partner = 2 * m + o
    x_right, x_left = (x + 1) % NX, (x + NX - 1) % NX

    def plane(chip):
        return {"ctx": 2 * chip + s}

    barrier = pltpu.get_barrier_semaphore()

    def greet(i, carry):
        pl.semaphore_signal(barrier, inc=1, device_id=plane((m + i) % CHIPS), device_id_type=MESH)
        return carry

    lax.fori_loop(1, CHIPS, greet, 0)
    pl.semaphore_signal(barrier, inc=1, device_id={"ctx": partner}, device_id_type=MESH)
    pl.semaphore_signal(barrier, inc=1, device_id={"ch": x_right}, device_id_type=MESH)
    pl.semaphore_signal(barrier, inc=1, device_id={"ch": x_left}, device_id_type=MESH)

    def remote(src, dst, send, recv, device):
        return pltpu.make_async_remote_copy(
            src_ref=src, dst_ref=dst, send_sem=send, recv_sem=recv,
            device_id=device, device_id_type=MESH,
        )

    def arrived(ref, sem):
        pltpu.make_async_copy(ref, ref, sem).wait()

    for j in range(WIDTH // 128):
        lanes = slice(128 * j, 128 * j + 128)
        rows = slice(8 * j, 8 * j + 8)
        tf[rows] = lf_ref[:, lanes].T.reshape(8, 2, OWN, TOK)
    exf_out[...] = tf[:, o].reshape(CHIPS * OWN, TOK).astype(BF16)
    for j in range(WIDTH // 128):
        lanes = slice(128 * j, 128 * j + 128)
        rows = slice(8 * j, 8 * j + 8)
        tp[rows] = (k_ref[:, lanes].astype(F32) * v_ref[:, lanes].astype(F32)).T.reshape(8, 2, OWN, TOK)
        tq[rows] = q_ref[:, lanes].astype(F32).T.reshape(8, 2, OWN, TOK)
    exp_out[0] = tp[:, o].reshape(CHIPS * OWN, TOK).astype(BF16)
    exp_out[1] = tq[:, o].reshape(CHIPS * OWN, TOK).astype(BF16)

    pl.semaphore_wait(barrier, CHIPS + 2)

    swap_f = remote(exf_out, exf_in, ex_send.at[0], ex_recv.at[0], {"ctx": partner})
    swap_p = remote(exp_out, exp_in, ex_send.at[1], ex_recv.at[1], {"ctx": partner})
    swap_f.start()
    swap_p.start()

    swap_f.wait()
    tf[:, o] = exf_in[...].astype(F32).reshape(CHIPS, OWN, TOK)
    send_f[...] = tf[...].reshape(CHIPS, 2 * OWN, TOK).astype(BF16)

    def spread(src, dst, which):
        pltpu.make_async_copy(src.at[m], dst.at[m], a_recv.at[which]).start()

        def one(i, carry):
            chip = (m + i) % CHIPS
            remote(src.at[chip], dst.at[m], a_send.at[which], a_recv.at[which], plane(chip)).start()
            return carry

        lax.fori_loop(1, CHIPS, one, 0)

    def gathered(src, dst, which):
        arrived(dst, a_recv.at[which])
        arrived(src.at[pl.ds(0, CHIPS - 1)], a_send.at[which])

    spread(send_f, recv_f, 0)
    swap_p.wait()
    tp[:, o] = exp_in[0].astype(F32).reshape(CHIPS, OWN, TOK)
    tq[:, o] = exp_in[1].astype(F32).reshape(CHIPS, OWN, TOK)
    send_pq[:, : 2 * OWN] = tp[...].reshape(CHIPS, 2 * OWN, TOK).astype(BF16)
    send_pq[:, 2 * OWN :] = tq[...].reshape(CHIPS, 2 * OWN, TOK).astype(BF16)
    spread(send_pq, recv_pq, 1)

    for h in range(2):
        pltpu.make_async_copy(wt_ref.at[pl.ds(16 * h, 16)], wall.at[y, z, s, h], w1_recv.at[h]).start()
    for i in range(1, 8):
        remote(
            wt_ref.at[pl.ds(0, 16)], wall.at[y, z, s, 0], w1_send, w1_recv.at[0],
            plane(y * NZ + (z + i) % NZ),
        ).start()
        remote(
            wt_ref.at[pl.ds(16, 16)], wall.at[y, z, s, 1], w1_send, w1_recv.at[1],
            plane((y + i) % NY * NZ + z),
        ).start()

    y_right, y_left = (y + 1) % NY, (y + NY - 1) % NY
    z_right, z_left = (z + 1) % NZ, (z + NZ - 1) % NZ

    def chunk(h, offset, part=None):
        span = slice(None) if part is None else pl.ds(4 * part, 4)
        if h == 0:
            return wall.at[(y + offset + NY) % NY, span, s, 0]
        return wall.at[span, (z + offset + NZ) % NZ, s, 1]

    def toward(h, right):
        if h == 0:
            return plane((y_right if right else y_left) * NZ + z)
        return plane(y * NZ + (z_right if right else z_left))

    def share(ref):
        remote(ref, ref, wp_send, wp_recv, {"ctx": partner}).start()

    def weight_step(j):
        for h in range(2):
            if j == 0:
                arrived(chunk(h, 0), w1_recv.at[h])
                share(chunk(h, 0))
            elif j < 4:
                arrived(chunk(h, -j), w2_recv.at[h, 0, j - 1])
                arrived(chunk(h, j), w2_recv.at[h, 1, j - 1])
            else:
                arrived(chunk(h, 4, 0), w2_recv.at[h, 0, 3])
                arrived(chunk(h, 4, 1), w2_recv.at[h, 1, 3])
                share(chunk(h, 4))
            if j < 4:
                part_right, part_left = (0, 1) if j == 3 else (None, None)
                right, left = chunk(h, -j, part_right), chunk(h, j, part_left)
                remote(right, right, w2_send, w2_recv.at[h, 0, j], toward(h, True)).start()
                remote(left, left, w2_send, w2_recv.at[h, 1, j], toward(h, False)).start()
            if 0 < j < 4:
                share(chunk(h, -j))
                share(chunk(h, j))

    taps_t[...] = sf_ref[:, pl.ds(pl.multiple_of(me // 16 * 128, 128), 128)].T

    def forward(signal):
        stage = dot(first_ref[...], jnp.concatenate([signal, signal], 0))
        real, imag = stage[:TOK], stage[TOK:]
        turn_real, turn_imag = turn_ref[0], turn_ref[1]
        turned = jnp.concatenate(
            [real * turn_real - imag * turn_imag, real * turn_imag + imag * turn_real], 1
        )
        high, low = halves(turned)
        return dot(high, second_ref[0]) + dot(low, second_ref[0]) + dot(high, second_ref[1])

    def toeplitz(c, carry):
        row = taps_t[pl.ds(me % 16 * OWN + c, 1), :]
        base = jnp.concatenate([row, jnp.zeros_like(row)], 1)
        square = pltpu.roll(jnp.broadcast_to(base, (TOK, 2 * TOK)), 0, 1, stride=1, stride_axis=0)
        high, low = halves(square)
        toep[c] = jnp.concatenate([high, low], 0)
        return carry

    lax.fori_loop(0, OWN, toeplitz, 0)

    gathered(send_f, recv_f, 0)
    flat_f = tf.reshape(CHIPS * 2 * OWN, TOK)
    flat_p = tp.reshape(CHIPS * 2 * OWN, TOK)
    flat_q = tq.reshape(CHIPS * 2 * OWN, TOK)
    flat_y = ys.reshape(CHIPS * 2 * OWN, TOK)
    flat_f[...] = recv_f[...].astype(F32).reshape(CHIPS * 2 * OWN, TOK)

    def filter_spectrum(c, carry):
        spectrum[c] = forward(flat_f[pl.ds(c, TOK, stride=OWN), :].astype(BF16))
        return carry

    lax.fori_loop(0, OWN, filter_spectrum, 0)
    weight_step(0)

    gathered(send_pq, recv_pq, 1)
    flat_p[...] = recv_pq[:, : 2 * OWN].astype(F32).reshape(CHIPS * 2 * OWN, TOK)
    flat_q[...] = recv_pq[:, 2 * OWN :].astype(F32).reshape(CHIPS * 2 * OWN, TOK)

    def convolve(c, carry):
        product = flat_p[pl.ds(c, TOK, stride=OWN), :].astype(BF16)
        query = flat_q[pl.ds(c, TOK, stride=OWN), :]
        spread_out = dot(jnp.concatenate([product, product], 1), toep[c])
        spill = pltpu.roll(spread_out[:, TOK:], 1, 0)
        rows = lax.broadcasted_iota(jnp.int32, (TOK, TOK), 0)
        short_mix = spread_out[:, :TOK] + jnp.where(rows == 0, 0.0, spill)
        gated = (query * short_mix).astype(BF16)
        signal = forward(gated)
        other = spectrum[c]
        real, imag = signal[:, :TOK], signal[:, TOK:]
        other_real, other_imag = other[:, :TOK], other[:, TOK:]
        joint = jnp.concatenate(
            [real * other_real - imag * other_imag, real * other_imag + imag * other_real], 1
        )
        high, low = halves(joint)
        mixed = dot(high, third_ref[0]) + dot(low, third_ref[0]) + dot(high, third_ref[1])
        real, imag = mixed[:, :TOK], mixed[:, TOK:]
        turn_real, turn_imag = turn_ref[0], turn_ref[1]
        back = jnp.concatenate(
            [real * turn_real + imag * turn_imag, imag * turn_real - real * turn_imag], 0
        )
        high, low = halves(back)
        flat_y[pl.ds(c, TOK, stride=OWN), :] = (
            dot(last_ref[0], high) + dot(last_ref[0], low) + dot(last_ref[1], high)
        )
        return carry

    lax.fori_loop(0, OWN // 2, convolve, 0)
    weight_step(1)
    lax.fori_loop(OWN // 2, OWN, convolve, 0)

    exr_out[...] = ys[:, o].reshape(CHIPS * OWN, TOK).astype(BF16)
    swap_r = remote(exr_out, exr_in, ex_send.at[2], ex_recv.at[2], {"ctx": partner})
    swap_r.start()
    swap_r.wait()
    ys[:, o] = exr_in[...].astype(F32).reshape(CHIPS, OWN, TOK)
    send_r[...] = ys[...].reshape(CHIPS, 2 * OWN, TOK).astype(BF16)
    spread(send_r, recv_r, 2)
    weight_step(2)
    gathered(send_r, recv_r, 2)

    for j in range(WIDTH // 128):
        lanes = slice(128 * j, 128 * j + 128)
        block = recv_r[8 * j : 8 * j + 8].astype(F32).reshape(128, TOK).T
        hidden[:, lanes] = (v_ref[:, lanes].astype(F32) * block).astype(BF16)
    weight_step(3)
    weight_step(4)
    arrived(wall.at[:, :, o], wp_recv)

    def project(block, t):
        rows = wall[2 * block + t // 2, pl.ds(4 * (t % 2), 4)].reshape(256, WIDTH)
        return lax.dot_general(
            hidden[...], rows, (((1,), (1,)), ((), ())), preferred_element_type=F32
        )

    for t in range(4):
        hop_out[t // 2, :, 256 * (t % 2) : 256 * (t % 2) + 256] = project((x + 2) % NX, t).astype(BF16)
    hop_a = remote(hop_out.at[0], hop_in.at[0], x_send.at[0], x_recv.at[0], {"ch": x_right})
    hop_b = remote(hop_out.at[1], hop_in.at[1], x_send.at[1], x_recv.at[1], {"ch": x_left})
    hop_a.start()
    hop_b.start()
    for t in range(4):
        part_r[t // 2, :, 256 * (t % 2) : 256 * (t % 2) + 256] = project(x_right, t)
        part_l[t // 2, :, 256 * (t % 2) : 256 * (t % 2) + 256] = project(x_left, t)
    right_out[1] = part_r[1].astype(BF16)
    left_out[0] = part_l[0].astype(BF16)
    hop_a.wait()
    right_out[0] = (part_r[0] + hop_in[0].astype(F32)).astype(BF16)
    hop_b.wait()
    left_out[1] = (part_l[1] + hop_in[1].astype(F32)).astype(BF16)
    go_right = remote(right_out, from_left, x_send.at[2], x_recv.at[2], {"ch": x_right})
    go_left = remote(left_out, from_right, x_send.at[3], x_recv.at[3], {"ch": x_left})
    go_right.start()
    go_left.start()
    for t in range(4):
        part_r[t // 2, :, 256 * (t % 2) : 256 * (t % 2) + 256] = project(x, t)
    go_right.wait()
    go_left.wait()
    for h in range(2):
        total = part_r[h] + from_left[h].astype(F32) + from_right[h].astype(F32)
        out_ref[:, 512 * h : 512 * h + 512] = total.astype(BF16)

    arrived(wall.at[0, pl.ds(0, 7), s], w1_send)
    arrived(wall.at[pl.ds(0, 7), :, s], w2_send)
    arrived(wall.at[:, :, s], wp_send)


def local(query_act, key_act, value_act, short_filter, long_filter, out_weight):
    tables = make_tables()
    vmem = pl.BlockSpec(memory_space=pltpu.VMEM)
    rows = CHIPS * OWN
    block_f32 = pltpu.VMEM((CHIPS, 2, OWN, TOK), F32)
    half_bf16 = pltpu.VMEM((rows, TOK), BF16)
    pair_bf16 = pltpu.VMEM((2, rows, TOK), BF16)
    tiles = pltpu.VMEM((CHIPS, 2 * OWN, TOK), BF16)
    wide_tiles = pltpu.VMEM((CHIPS, 4 * OWN, TOK), BF16)
    share_bf16 = pltpu.VMEM((2, TOK, WIDTH // 2), BF16)
    share_f32 = pltpu.VMEM((2, TOK, WIDTH // 2), F32)
    dma = pltpu.SemaphoreType.DMA
    return pl.pallas_call(
        kernel,
        out_shape=jax.ShapeDtypeStruct((TOK, WIDTH), BF16),
        in_specs=[vmem] * (6 + len(tables)),
        out_specs=vmem,
        scratch_shapes=[
            block_f32, block_f32, block_f32, block_f32, pltpu.VMEM((TOK, 128), F32),
            half_bf16, half_bf16, pair_bf16, pair_bf16, half_bf16, half_bf16,
            tiles, tiles, wide_tiles, wide_tiles, tiles, tiles,
            pltpu.VMEM((OWN, 2 * TOK, 2 * TOK), BF16),
            pltpu.VMEM((OWN, TOK, 2 * TOK), F32),
            pltpu.VMEM((NY, NZ, 2, 2, 16, WIDTH), BF16),
            pltpu.VMEM((TOK, WIDTH), BF16),
            share_bf16, share_bf16, share_bf16, share_bf16, share_bf16, share_bf16,
            share_f32, share_f32,
            dma((3,)), dma((3,)), dma((3,)), dma((3,)), dma, dma((2,)), dma, dma((2, 2, 4)), dma, dma,
            dma((4,)), dma((4,)),
        ],
        compiler_params=pltpu.CompilerParams(
            collective_id=0, has_side_effects=True, vmem_limit_bytes=48 * 1024 * 1024
        ),
    )(query_act, key_act, value_act, short_filter, long_filter, out_weight.T, *tables)


def solution(mesh):
    placed = (
        P("ctx", "ch"),
        P("ctx", "ch"),
        P("ctx", "ch"),
        P(None, "ch"),
        P("ctx", "ch"),
        P("ch", "ctx"),
    )
    return jax.shard_map(
        local, mesh=mesh, in_specs=placed, out_specs=P("ctx", "ch"), check_vma=False
    )
```

profile of v0, /device:TPU:1, one launch (start us, length us, event | category | flops | bytes accessed | tf_op | source)
XLA Modules:
  0.0 103.9 jit_solution(12800622535993390300)
XLA Ops:
  0.0 0.0 copy-start
  0.0 1.0 %copy-done = f32[128,1024]{1,0:T(8,128)S(1)} copy-done((f32[128,1024]{1,0:T(8,128)S(1)}, f32[128,1024]{1,0:T(8,128)}, u32[]{:S(2)}) %copy-start) | copy-done | bytes 524312
  1.0 0.0 copy-start.1
  1.0 1.0 %copy-done.1 = f32[128,1024]{1,0:T(8,128)S(1)} copy-done((f32[128,1024]{1,0:T(8,128)S(1)}, f32[128,1024]{1,0:T(8,128)}, u32[]{:S(2)}) %copy-start.1) | copy-done | bytes 524312
  2.1 0.0 copy-start.2
  2.1 0.9 copy-done.2
  3.0 0.0 copy-start.3
  3.0 0.9 copy-done.3
  4.0 0.0 copy-start.4
  4.0 0.9 copy-done.4
  4.9 0.0 copy-start.5
  4.9 0.9 copy-done.5
  5.9 0.0 copy-start.6
  5.9 0.9 copy-done.6
  6.8 0.0 copy-start.7
  6.8 0.9 copy-done.7
  7.7 0.0 copy-start.8
  7.7 0.9 copy-done.8
  8.6 0.0 copy-start.9
  8.6 0.9 copy-done.9
  9.6 0.0 copy-start.10
  9.6 0.8 copy-done.10
  10.4 92.8 %shard_map.109 = bf16[128,1024]{1,0:T(8,128)(2,1)S(1)} custom-call(bf16[128,1024]{1,0:T(8,128)(2,1)S(1)} %copy-done.2, bf16[128,1024]{1,0:T(8,128)(2,1)S(1)} %copy-done.3, bf16[128,1024]{1,0:T(8,128)(2,1)S(1)} %copy-done.4, f32[128,1024]{1,0:T(8,128)S(1)} %copy-done, f32[128,1024]{1,0:T(8,128)S(1)} %copy-done.1, bf16[32,1024]{1,0:T(8,128)(2,1)S(1)} %bitcast.1, ...), custom_call_target="tpu_custom_call" | custom-call | tf_op jit(solution)/shard_map/pallas_call | solution.py:338
  103.2 0.7 copy.13
Async XLA Ops:
  0.0 1.0 %copy-start = (f32[128,1024]{1,0:T(8,128)S(1)}, f32[128,1024]{1,0:T(8,128)}, u32[]{:S(2)}) copy-start(f32[128,1024]{1,0:T(8,128)} %sf_ref.1) | copy-start | bytes 1572868
  1.0 1.0 %copy-start.1 = (f32[128,1024]{1,0:T(8,128)S(1)}, f32[128,1024]{1,0:T(8,128)}, u32[]{:S(2)}) copy-start(f32[128,1024]{1,0:T(8,128)} %lf_ref.1) | copy-start | bytes 1572868
  2.1 0.9 copy-start.2
  3.0 0.9 copy-start.3
  4.0 0.9 copy-start.4
  4.9 0.9 copy-start.5
  5.9 0.9 copy-start.6
  6.8 0.9 copy-start.7
  7.7 0.9 copy-start.8
  8.6 0.9 copy-start.9
  9.6 0.8 copy-start.10
where the time goes:
time: 104 us
  Pallas kernels  92.8 us (89%)
  local copies, waits for them, and re-layouts  11.1 us (11%)
    pallas_call x1, Pallas kernels, local(): pl.pallas_call(kernel, out_shape=jax.ShapeDtypeStruct((TOK, WIDTH), BF16)...  92.8 us
    unnamed x23, local copies, waits for them, and re-layouts  11.1 us

commit v1 on v0

v1 whole, which is shorter than its diff:
```python
import math

import jax
import jax.numpy as jnp
import numpy as np
from jax import lax
from jax.experimental import pallas as pl
from jax.experimental.pallas import tpu as pltpu
from jax.sharding import PartitionSpec as P

NX, NY, NZ = 4, 8, 8
CHIPS = NY * NZ
TOK = 128
WIDTH = 1024
OWN = 8
MESH = pl.DeviceIdType.MESH
F32, BF16 = jnp.float32, jnp.bfloat16


def split_table(table):
    high = table.astype(jnp.bfloat16)
    low = (table - high.astype(np.float64)).astype(jnp.bfloat16)
    return high, low


def make_tables():
    blocks = 2 * CHIPS
    half_odd = np.arange(blocks) + 0.5
    index = np.arange(blocks)
    angle = 2 * math.pi * half_odd[:, None] * index[None, :] / (2 * blocks)
    first = np.concatenate([np.cos(angle), -np.sin(angle)], 0)
    fold = split_table(first)
    first_cat = np.concatenate(fold, 1)
    last = split_table(first.T * (2.0 / (2 * blocks * TOK)))
    inner = 2 * math.pi * (np.arange(TOK)[:, None] * np.arange(TOK)[None, :] % TOK) / TOK
    cosine, minus_sine = np.cos(inner), -np.sin(inner)
    second = np.block([[cosine, minus_sine], [-minus_sine, cosine]])
    second_split = split_table(second)
    third_split = split_table(second.T)
    turn = 2 * math.pi * half_odd[:, None] * np.arange(TOK)[None, :] / (2 * blocks * TOK)
    order = np.zeros((512, 512))
    column = np.arange(512)
    order[column // 16 % 2 * 256 + column // 32 * 16 + column % 16, column] = 1.0
    return (
        first_cat,
        np.stack(last),
        np.stack(second_split),
        np.stack(third_split),
        np.stack([np.cos(turn), -np.sin(turn)]).astype(np.float32),
        order.astype(jnp.bfloat16),
    )


def dot(a, b):
    return jnp.dot(a, b, preferred_element_type=F32)


def halves(value):
    high = value.astype(BF16)
    return high, (value - high.astype(F32)).astype(BF16)


def kernel(
    q_hbm, k_hbm, v_hbm, sf_hbm, lf_hbm, wt_ref,
    first_hbm, last_hbm, second_hbm, third_hbm, turn_hbm, order_hbm,
    out_ref,
    q_ref, k_ref, v_ref, sf_ref, lf_ref,
    first_ref, last_ref, second_ref, third_ref, turn_ref, order_ref, load_sems,
    ext, short, halo_out, halo_in,
    tf, tg, ys,
    exf_out, exf_in, exg_out, exg_in, exr_out, exr_in,
    send_f, recv_f, send_g, recv_g, send_r, recv_r,
    spectrum, wall, hidden,
    hop_out, hop_in, right_out, left_out, from_left, from_right, part_r, part_l,
    ex_send, ex_recv, a_send, a_recv, w1_send, w1_recv, w2_send, w2_recv, wp_send, wp_recv,
    x_send, x_recv,
):
    me = lax.axis_index("ctx")
    x = lax.axis_index("ch")
    m, s = me // 2, me % 2
    o = 1 - s
    y, z = m // NZ, m % NZ
    partner = 2 * m + o
    after = (me + 1) % (2 * CHIPS)
    x_right, x_left = (x + 1) % NX, (x + NX - 1) % NX

    def plane(chip):
        return {"ctx": 2 * chip + s}

    loads = [
        pltpu.make_async_copy(src, dst, load_sems.at[i])
        for i, (src, dst) in enumerate([
            (k_hbm, k_ref), (v_hbm, v_ref), (lf_hbm, lf_ref), (sf_hbm, sf_ref), (q_hbm, q_ref),
            (first_hbm, first_ref), (second_hbm, second_ref), (turn_hbm, turn_ref),
            (third_hbm, third_ref), (last_hbm, last_ref), (order_hbm, order_ref),
        ])
    ]
    for load in loads:
        load.start()

    barrier = pltpu.get_barrier_semaphore()

    def greet(i, carry):
        pl.semaphore_signal(barrier, inc=1, device_id=plane((m + i) % CHIPS), device_id_type=MESH)
        return carry

    lax.fori_loop(1, CHIPS, greet, 0)
    other_chip = (m + 2 * s - 1 + CHIPS) % CHIPS
    for device in (
        {"ctx": partner}, {"ctx": 2 * other_chip + o}, {"ch": x_right}, {"ch": x_left},
    ):
        pl.semaphore_signal(barrier, inc=1, device_id=device, device_id_type=MESH)

    def remote(src, dst, send, recv, device):
        return pltpu.make_async_remote_copy(
            src_ref=src, dst_ref=dst, send_sem=send, recv_sem=recv,
            device_id=device, device_id_type=MESH,
        )

    def arrived(ref, sem):
        pltpu.make_async_copy(ref, ref, sem).wait()

    y_right, y_left = (y + 1) % NY, (y + NY - 1) % NY
    z_right, z_left = (z + 1) % NZ, (z + NZ - 1) % NZ

    def half_lanes(h):
        return pl.ds(512 * h, 512)

    def chunk(h, offset, r, part=None):
        span = slice(None) if part is None else pl.ds(4 * part, 4)
        if h == 0:
            return wall.at[(y + offset + NY) % NY, span, s, r, :, half_lanes(h)]
        return wall.at[span, (z + offset + NZ) % NZ, s, r, :, half_lanes(h)]

    def toward(h, right):
        if h == 0:
            return plane((y_right if right else y_left) * NZ + z)
        return plane(y * NZ + (z_right if right else z_left))

    def share(ref, r):
        remote(ref, ref, wp_send, wp_recv.at[r], {"ctx": partner}).start()

    def weight_start():
        for r in range(2):
            for h in range(2):
                src = wt_ref.at[pl.ds(16 * r, 16), half_lanes(h)]
                dst = wall.at[y, z, s, r, :, half_lanes(h)]
                pltpu.make_async_copy(src, dst, w1_recv.at[r, h]).start()
                for i in range(1, 8):
                    chip = y * NZ + (z + i) % NZ if h == 0 else (y + i) % NY * NZ + z
                    remote(src, dst, w1_send, w1_recv.at[r, h], plane(chip)).start()

    def weight_step(j, r):
        for h in range(2):
            if j == 0:
                arrived(chunk(h, 0, r), w1_recv.at[r, h])
                share(chunk(h, 0, r), r)
            elif j < 4:
                arrived(chunk(h, -j, r), w2_recv.at[h, 0, j - 1, r])
                arrived(chunk(h, j, r), w2_recv.at[h, 1, j - 1, r])
            else:
                arrived(chunk(h, 4, r, 0), w2_recv.at[h, 0, 3, r])
                arrived(chunk(h, 4, r, 1), w2_recv.at[h, 1, 3, r])
                share(chunk(h, 4, r), r)
            if j < 4:
                for side in range(2):
                    moved = chunk(h, j if side else -j, r, side if j == 3 else None)
                    remote(
                        moved, moved, w2_send, w2_recv.at[h, side, j, r], toward(h, side == 0)
                    ).start()
            if 0 < j < 4:
                share(chunk(h, -j, r), r)
                share(chunk(h, j, r), r)

    loads[0].wait()
    loads[1].wait()
    for j in range(WIDTH // 128):
        lanes = slice(128 * j, 128 * j + 128)
        product = k_ref[:, lanes].astype(F32) * v_ref[:, lanes].astype(F32)
        ext[j, TOK:] = product
        halo_out[j] = product.astype(BF16)

    loads[2].wait()
    for j in range(WIDTH // 128):
        lanes = slice(128 * j, 128 * j + 128)
        tf[8 * j : 8 * j + 8] = lf_ref[:, lanes].T.reshape(8, 2, OWN, TOK)
    exf_out[...] = tf[:, o].reshape(CHIPS * OWN, TOK).astype(BF16)
    loads[3].wait()

    def short_part(j, prior):
        lanes = pl.ds(pl.multiple_of(j * 128, 128), 128)
        if prior:
            accum = [short[j, 8 * i : 8 * i + 8] for i in range(16)]
        else:
            accum = [jnp.zeros((8, 128), F32) for i in range(16)]
        for r in range(8):
            ranks = range(1, 17) if prior else range(17, 32)
            windows = {u: ext[j, 8 * u - r : 8 * u - r + 8] for u in ranks}
            for q in range(16):
                taps = jnp.broadcast_to(sf_ref[8 * q + r : 8 * q + r + 1, lanes], (8, 128))
                for i in range(0, q + 1) if prior else range(q + 1, 16):
                    accum[i] = accum[i] + taps * windows[i - q + 16]
        for i in range(16):
            short[j, 8 * i : 8 * i + 8] = accum[i]

    def short_own(j, carry):
        short_part(j, False)
        return carry

    def short_prior(j, carry):
        short_part(j, True)
        return carry

    lax.fori_loop(0, WIDTH // 128, short_own, 0)

    pl.semaphore_wait(barrier, CHIPS + 3)

    halo = remote(halo_out, halo_in, ex_send.at[1], ex_recv.at[1], {"ctx": after})
    halo.start()
    weight_start()

    swap_f = remote(exf_out, exf_in, ex_send.at[0], ex_recv.at[0], {"ctx": partner})
    swap_f.start()

    def spread(src, dst, which):
        pltpu.make_async_copy(src.at[m], dst.at[m], a_recv.at[which]).start()

        def one(i, carry):
            chip = (m + i) % CHIPS
            remote(src.at[chip], dst.at[m], a_send.at[which], a_recv.at[which], plane(chip)).start()
            return carry

        lax.fori_loop(1, CHIPS, one, 0)

    def gathered(src, dst, which):
        arrived(dst, a_recv.at[which])
        arrived(src.at[pl.ds(0, CHIPS - 1)], a_send.at[which])

    swap_f.wait()
    tf[:, o] = exf_in[...].astype(F32).reshape(CHIPS, OWN, TOK)
    send_f[...] = tf[...].reshape(CHIPS, 2 * OWN, TOK).astype(BF16)
    spread(send_f, recv_f, 0)
    halo.wait()
    loads[4].wait()
    first_device = me == 0
    for j in range(WIDTH // 128):
        ext[j, :TOK] = jnp.where(first_device, 0.0, halo_in[j].astype(F32))
    lax.fori_loop(0, WIDTH // 128, short_prior, 0)
    for j in range(WIDTH // 128):
        lanes = slice(128 * j, 128 * j + 128)
        tg[8 * j : 8 * j + 8] = (q_ref[:, lanes].astype(F32) * short[j]).T.reshape(8, 2, OWN, TOK)
    exg_out[...] = tg[:, o].reshape(CHIPS * OWN, TOK).astype(BF16)
    swap_g = remote(exg_out, exg_in, ex_send.at[3], ex_recv.at[3], {"ctx": partner})
    swap_g.start()
    weight_step(0, 0)
    swap_g.wait()
    tg[:, o] = exg_in[...].astype(F32).reshape(CHIPS, OWN, TOK)
    send_g[...] = tg[...].reshape(CHIPS, 2 * OWN, TOK).astype(BF16)
    spread(send_g, recv_g, 1)
    weight_step(0, 1)
    for load in loads[5:]:
        load.wait()
    flat_f = tf.reshape(CHIPS * 2 * OWN, TOK)
    flat_g = tg.reshape(CHIPS * 2 * OWN, TOK)
    flat_y = ys.reshape(CHIPS * 2 * OWN, TOK)

    def tile(value, c):
        return value[:, TOK * c : TOK * c + TOK]

    def times(value, table):
        high, low = halves(value)
        return dot(high, table[0]) + dot(low, table[0]) + dot(high, table[1])

    def forward(flat, base):
        signal = jnp.concatenate(
            [flat[pl.ds(base + c, TOK, stride=OWN), :].astype(BF16) for c in range(4)], 1
        )
        stage = dot(first_ref[...], jnp.concatenate([signal, signal], 0))
        turn_real, turn_imag = turn_ref[0], turn_ref[1]
        turned = []
        for c in range(4):
            real, imag = tile(stage[:TOK], c), tile(stage[TOK:], c)
            turned.append(jnp.concatenate(
                [real * turn_real - imag * turn_imag, real * turn_imag + imag * turn_real], 1
            ))
        return times(jnp.concatenate(turned, 0), second_ref)

    gathered(send_f, recv_f, 0)
    flat_f[...] = recv_f[...].astype(F32).reshape(CHIPS * 2 * OWN, TOK)
    for g in range(2):
        spectrum[g] = forward(flat_f, 4 * g)
    weight_step(1, 0)
    gathered(send_g, recv_g, 1)
    flat_g[...] = recv_g[...].astype(F32).reshape(CHIPS * 2 * OWN, TOK)

    def convolve(g):
        signal = forward(flat_g, 4 * g)
        other = spectrum[g]
        real, imag = tile(signal, 0), tile(signal, 1)
        other_real, other_imag = tile(other, 0), tile(other, 1)
        joint = jnp.concatenate(
            [real * other_real - imag * other_imag, real * other_imag + imag * other_real], 1
        )
        mixed = times(joint, third_ref)
        turn_real, turn_imag = turn_ref[0], turn_ref[1]
        back = []
        for c in range(4):
            rows = mixed[TOK * c : TOK * c + TOK]
            real, imag = tile(rows, 0), tile(rows, 1)
            back.append(jnp.concatenate(
                [real * turn_real + imag * turn_imag, imag * turn_real - real * turn_imag], 0
            ))
        high, low = halves(jnp.concatenate(back, 1))
        result = dot(last_ref[0], high) + dot(last_ref[0], low) + dot(last_ref[1], high)
        for c in range(4):
            flat_y[pl.ds(4 * g + c, TOK, stride=OWN), :] = tile(result, c)

    weight_step(1, 1)
    convolve(0)
    weight_step(2, 0)
    convolve(1)
    weight_step(2, 1)
    exr_out[...] = ys[:, o].reshape(CHIPS * OWN, TOK).astype(BF16)
    swap_r = remote(exr_out, exr_in, ex_send.at[2], ex_recv.at[2], {"ctx": partner})
    swap_r.start()
    swap_r.wait()
    ys[:, o] = exr_in[...].astype(F32).reshape(CHIPS, OWN, TOK)
    send_r[...] = ys[...].reshape(CHIPS, 2 * OWN, TOK).astype(BF16)
    spread(send_r, recv_r, 2)
    weight_step(3, 0)
    gathered(send_r, recv_r, 2)
    weight_step(3, 1)
    for j in range(WIDTH // 128):
        lanes = slice(128 * j, 128 * j + 128)
        block = recv_r[8 * j : 8 * j + 8].astype(F32).reshape(128, TOK).T
        hidden[:, lanes] = (v_ref[:, lanes].astype(F32) * block).astype(BF16)
    weight_step(4, 0)
    def project(block, t, r):
        rows = wall[2 * block + t, :, :, r].reshape(256, WIDTH)
        return lax.dot_general(
            hidden[...], rows, (((1,), (1,)), ((), ())), preferred_element_type=F32
        )

    def hop(r, t):
        return remote(
            hop_out.at[r, t], hop_in.at[r, t], x_send.at[r, t], x_recv.at[r, t],
            {"ch": x_left if t else x_right},
        )

    def share_of(r, side):
        return remote(
            left_out.at[r] if side else right_out.at[r],
            from_right.at[r] if side else from_left.at[r],
            x_send.at[r, 2 + side], x_recv.at[r, 2 + side], {"ch": x_left if side else x_right},
        )

    def far(r):
        for t in range(2):
            hop_out[r, t] = project((x + 2) % NX, t, r).astype(BF16)
            hop(r, t).start()

    def near(r):
        right_out[r, 1] = project(x_right, 1, r).astype(BF16)
        left_out[r, 0] = project(x_left, 0, r).astype(BF16)
        part_r[r] = project(x_right, 0, r)
        part_l[r] = project(x_left, 1, r)

    def onward(r):
        hop(r, 0).wait()
        right_out[r, 0] = (part_r[r] + hop_in[r, 0].astype(F32)).astype(BF16)
        share_of(r, 0).start()
        hop(r, 1).wait()
        left_out[r, 1] = (part_l[r] + hop_in[r, 1].astype(F32)).astype(BF16)
        share_of(r, 1).start()

    arrived(wall.at[:, :, o, 0], wp_recv.at[0])
    far(0)
    near(0)
    onward(0)
    weight_step(4, 1)
    arrived(wall.at[:, :, o, 1], wp_recv.at[1])
    far(1)
    near(1)
    mine = [[project(x, t, 0) for t in range(2)]]
    onward(1)
    mine.append([project(x, t, 1) for t in range(2)])
    for r in range(2):
        for side in range(2):
            share_of(r, side).wait()
    for t in range(2):
        pieces = [
            (mine[r][t] + from_left[r, t].astype(F32) + from_right[r, t].astype(F32)).astype(BF16)
            for r in range(2)
        ]
        out_ref[:, 512 * t : 512 * t + 512] = dot(jnp.concatenate(pieces, 1), order_ref[...]).astype(BF16)

    arrived(wall.at[0, pl.ds(0, 7), s], w1_send)
    arrived(wall.at[pl.ds(0, 7), :, s], w2_send)
    arrived(wall.at[:, :, s], wp_send)


def local(query_act, key_act, value_act, short_filter, long_filter, out_weight):
    tables = make_tables()
    vmem = pl.BlockSpec(memory_space=pltpu.VMEM)
    rows = CHIPS * OWN
    block_f32 = pltpu.VMEM((CHIPS, 2, OWN, TOK), F32)
    half_bf16 = pltpu.VMEM((rows, TOK), BF16)
    tiles = pltpu.VMEM((CHIPS, 2 * OWN, TOK), BF16)
    act = pltpu.VMEM((TOK, WIDTH), BF16)
    lane_tiles = pltpu.VMEM((WIDTH // 128, TOK, 128), BF16)
    share_bf16 = pltpu.VMEM((2, 2, TOK, 256), BF16)
    share_f32 = pltpu.VMEM((2, TOK, 256), F32)
    dma = pltpu.SemaphoreType.DMA
    return pl.pallas_call(
        kernel,
        out_shape=jax.ShapeDtypeStruct((TOK, WIDTH), BF16),
        in_specs=[pl.BlockSpec(memory_space=pl.ANY)] * (6 + len(tables)),
        out_specs=vmem,
        scratch_shapes=[
            act, act, act, pltpu.VMEM((TOK, WIDTH), F32), pltpu.VMEM((TOK, WIDTH), F32),
            *[pltpu.VMEM(table.shape, table.dtype) for table in tables], dma((11,)),
            pltpu.VMEM((WIDTH // 128, 2 * TOK, 128), F32), pltpu.VMEM((WIDTH // 128, TOK, 128), F32),
            lane_tiles, lane_tiles,
            block_f32, block_f32, block_f32,
            half_bf16, half_bf16, half_bf16, half_bf16, half_bf16, half_bf16,
            tiles, tiles, tiles, tiles, tiles, tiles,
            pltpu.VMEM((2, 4 * TOK, 2 * TOK), F32),
            pltpu.VMEM((NY, NZ, 2, 2, 16, WIDTH), BF16),
            act,
            share_bf16, share_bf16, share_bf16, share_bf16, share_bf16, share_bf16,
            share_f32, share_f32,
            dma((4,)), dma((4,)), dma((3,)), dma((3,)), dma, dma((2, 2)), dma, dma((2, 2, 4, 2)), dma, dma((2,)),
            dma((2, 4)), dma((2, 4)),
        ],
        compiler_params=pltpu.CompilerParams(
            collective_id=0, has_side_effects=True, vmem_limit_bytes=60 * 1024 * 1024
        ),
    )(query_act, key_act, value_act, short_filter, long_filter, out_weight.T, *tables)


def solution(mesh):
    placed = (
        P("ctx", "ch"),
        P("ctx", "ch"),
        P("ctx", "ch"),
        P(None, "ch"),
        P("ctx", "ch"),
        P("ch", "ctx"),
    )
    return jax.shard_map(
        local, mesh=mesh, in_specs=placed, out_specs=P("ctx", "ch"), check_vma=False
    )
```

time: 104 us -> 84.2 us (0.81)
  Pallas kernels: 92.8 us -> 82.4 us
  local copies, waits for them, and re-layouts: 11.1 us -> 1.67 us
    pallas_call x1, Pallas kernels: 92.8 us -> 82.4 us  [local(): pl.pallas_call(kernel, out_shape=jax.ShapeDtypeStruct((TOK, WIDTH), BF16)...]
    unnamed x23 -> x1, local copies, waits for them, and re-layouts: 11.1 us -> 1.67 us
where the time goes in v1:
time: 84.2 us; the launch traced here: 84.1 us
  Pallas kernels  82.4 us (98%)
  local copies, waits for them, and re-layouts  1.67 us (2%)
    pallas_call x1, Pallas kernels, local(): pl.pallas_call(kernel, out_shape=jax.ShapeDtypeStruct((TOK, WIDTH), BF16)...  82.4 us

profile of v1, /device:TPU:1, one launch (start us, length us, event | category | flops | bytes accessed | tf_op | source)
XLA Modules:
  0.0 84.1 jit_solution(7565168726579080685)
XLA Ops:
  0.0 82.4 %shard_map.118 = bf16[128,1024]{1,0:T(8,128)(2,1)} custom-call(bf16[128,1024]{1,0:T(8,128)(2,1)} %q_hbm.1, bf16[128,1024]{1,0:T(8,128)(2,1)} %k_hbm.1, bf16[128,1024]{1,0:T(8,128)(2,1)} %v_hbm.1, f32[128,1024]{1,0:T(8,128)} %sf_hbm.1, f32[128,1024]{1,0:T(8,128)} %lf_hbm.1, bf16[32,1024]{1,0:T(8,128)(2,1)} %bitcast.1, ...), custom_call_target="tpu_custom_call" | custom-call | tf_op jit(solution)/shard_map/pallas_call | solution.py:414
  82.4 1.7 %copy.14 = bf16[128,1024]{1,0:T(8,128)(2,1)} copy(bf16[128,1024]{1,0:T(8,128)(2,1)} %shard_map.118) | data formatting | bytes 524288

commit v2 on v1

--- a/solution.py
+++ b/solution.py
@@ -40,7 +40,8 @@
     turn = 2 * math.pi * half_odd[:, None] * np.arange(TOK)[None, :] / (2 * blocks * TOK)
     order = np.zeros((512, 512))
     column = np.arange(512)
-    order[column // 16 % 2 * 256 + column // 32 * 16 + column % 16, column] = 1.0
+    lane = column // 16 % 2 * 256 + column // 32 % 2 * 128 + column // 64 * 16 + column % 16
+    order[lane, column] = 1.0
     return (
         first_cat,
         np.stack(last),
@@ -123,14 +124,16 @@
     y_right, y_left = (y + 1) % NY, (y + NY - 1) % NY
     z_right, z_left = (z + 1) % NZ, (z + NZ - 1) % NZ
 
-    def half_lanes(h):
-        return pl.ds(512 * h, 512)
-
     def chunk(h, offset, r, part=None):
         span = slice(None) if part is None else pl.ds(4 * part, 4)
         if h == 0:
-            return wall.at[(y + offset + NY) % NY, span, s, r, :, half_lanes(h)]
-        return wall.at[span, (z + offset + NZ) % NZ, s, r, :, half_lanes(h)]
+            return wall.at[s, r, 0, (y + offset + NY) % NY, span]
+        return wall.at[s, r, 1, span, (z + offset + NZ) % NZ]
+
+    def piece(h, offset, r):
+        if h == 0:
+            return wall.at[s, r, 0, y, (z + offset + NZ) % NZ]
+        return wall.at[s, r, 1, (y + offset + NY) % NY, z]
 
     def toward(h, right):
         if h == 0:
@@ -140,21 +143,32 @@
     def share(ref, r):
         remote(ref, ref, wp_send, wp_recv.at[r], {"ctx": partner}).start()
 
+    def beside(h, step):
+        if h == 0:
+            return plane(y * NZ + (z + step + NZ) % NZ)
+        return plane((y + step + NY) % NY * NZ + z)
+
     def weight_start():
         for r in range(2):
             for h in range(2):
-                src = wt_ref.at[pl.ds(16 * r, 16), half_lanes(h)]
-                dst = wall.at[y, z, s, r, :, half_lanes(h)]
-                pltpu.make_async_copy(src, dst, w1_recv.at[r, h]).start()
-                for i in range(1, 8):
-                    chip = y * NZ + (z + i) % NZ if h == 0 else (y + i) % NY * NZ + z
-                    remote(src, dst, w1_send, w1_recv.at[r, h], plane(chip)).start()
+                own, place = wt_ref.at[pl.ds(16 * r, 16), pl.ds(512 * h, 512)], piece(h, 0, r)
+                pltpu.make_async_copy(own, place, w1_recv.at[r, h, 0]).start()
+                for step, which in ((2, 1), (-2, 2), (1, 0), (-1, 0)):
+                    remote(own, place, w1_send, w1_recv.at[r, h, which], beside(h, step)).start()
+
+    def weight_relay():
+        for r in range(2):
+            for h in range(2):
+                for step, which, targets in ((-2, 1, (2, 1)), (2, 2, (-1,))):
+                    moved = piece(h, step, r)
+                    arrived(moved, w1_recv.at[r, h, which])
+                    for target in targets:
+                        remote(moved, moved, w1_send, w1_recv.at[r, h, 0], beside(h, target)).start()
 
     def weight_step(j, r):
         for h in range(2):
             if j == 0:
-                arrived(chunk(h, 0, r), w1_recv.at[r, h])
-                share(chunk(h, 0, r), r)
+                arrived(wall.at[s, r, h, 0, pl.ds(0, 6)], w1_recv.at[r, h, 0])
             elif j < 4:
                 arrived(chunk(h, -j, r), w2_recv.at[h, 0, j - 1, r])
                 arrived(chunk(h, j, r), w2_recv.at[h, 1, j - 1, r])
@@ -168,7 +182,9 @@
                     remote(
                         moved, moved, w2_send, w2_recv.at[h, side, j, r], toward(h, side == 0)
                     ).start()
-            if 0 < j < 4:
+            if j == 0:
+                share(chunk(h, 0, r), r)
+            elif j < 4:
                 share(chunk(h, -j, r), r)
                 share(chunk(h, j, r), r)
 
@@ -234,13 +250,13 @@
 
     def gathered(src, dst, which):
         arrived(dst, a_recv.at[which])
-        arrived(src.at[pl.ds(0, CHIPS - 1)], a_send.at[which])
-
-    swap_f.wait()
+
+    swap_f.wait_recv()
     tf[:, o] = exf_in[...].astype(F32).reshape(CHIPS, OWN, TOK)
     send_f[...] = tf[...].reshape(CHIPS, 2 * OWN, TOK).astype(BF16)
+    weight_relay()
     spread(send_f, recv_f, 0)
-    halo.wait()
+    halo.wait_recv()
     loads[4].wait()
     first_device = me == 0
     for j in range(WIDTH // 128):
@@ -253,7 +269,7 @@
     swap_g = remote(exg_out, exg_in, ex_send.at[3], ex_recv.at[3], {"ctx": partner})
     swap_g.start()
     weight_step(0, 0)
-    swap_g.wait()
+    swap_g.wait_recv()
     tg[:, o] = exg_in[...].astype(F32).reshape(CHIPS, OWN, TOK)
     send_g[...] = tg[...].reshape(CHIPS, 2 * OWN, TOK).astype(BF16)
     spread(send_g, recv_g, 1)
@@ -323,7 +339,7 @@
     exr_out[...] = ys[:, o].reshape(CHIPS * OWN, TOK).astype(BF16)
     swap_r = remote(exr_out, exr_in, ex_send.at[2], ex_recv.at[2], {"ctx": partner})
     swap_r.start()
-    swap_r.wait()
+    swap_r.wait_recv()
     ys[:, o] = exr_in[...].astype(F32).reshape(CHIPS, OWN, TOK)
     send_r[...] = ys[...].reshape(CHIPS, 2 * OWN, TOK).astype(BF16)
     spread(send_r, recv_r, 2)
@@ -336,9 +352,12 @@
         hidden[:, lanes] = (v_ref[:, lanes].astype(F32) * block).astype(BF16)
     weight_step(4, 0)
     def project(block, t, r):
-        rows = wall[2 * block + t, :, :, r].reshape(256, WIDTH)
-        return lax.dot_general(
-            hidden[...], rows, (((1,), (1,)), ((), ())), preferred_element_type=F32
+        return sum(
+            lax.dot_general(
+                hidden[:, 512 * h : 512 * h + 512], wall[:, r, h, 2 * block + t].reshape(256, 512),
+                (((1,), (1,)), ((), ())), preferred_element_type=F32,
+            )
+            for h in range(2)
         )
 
     def hop(r, t):
@@ -347,11 +366,11 @@
             {"ch": x_left if t else x_right},
         )
 
-    def share_of(r, side):
+    def share_of(r, side, t):
         return remote(
-            left_out.at[r] if side else right_out.at[r],
-            from_right.at[r] if side else from_left.at[r],
-            x_send.at[r, 2 + side], x_recv.at[r, 2 + side], {"ch": x_left if side else x_right},
+            (left_out if side else right_out).at[r, t], (from_right if side else from_left).at[r, t],
+            x_send.at[r, 2 + 2 * side + t], x_recv.at[r, 2 + 2 * side + t],
+            {"ch": x_left if side else x_right},
         )
 
     def far(r):
@@ -361,42 +380,60 @@
 
     def near(r):
         right_out[r, 1] = project(x_right, 1, r).astype(BF16)
+        share_of(r, 0, 1).start()
         left_out[r, 0] = project(x_left, 0, r).astype(BF16)
+        share_of(r, 1, 0).start()
         part_r[r] = project(x_right, 0, r)
         part_l[r] = project(x_left, 1, r)
 
     def onward(r):
-        hop(r, 0).wait()
+        hop(r, 0).wait_recv()
         right_out[r, 0] = (part_r[r] + hop_in[r, 0].astype(F32)).astype(BF16)
-        share_of(r, 0).start()
-        hop(r, 1).wait()
+        share_of(r, 0, 0).start()
+        hop(r, 1).wait_recv()
         left_out[r, 1] = (part_l[r] + hop_in[r, 1].astype(F32)).astype(BF16)
-        share_of(r, 1).start()
-
-    arrived(wall.at[:, :, o, 0], wp_recv.at[0])
+        share_of(r, 1, 1).start()
+
+    def total_of(r, own):
+        for side in range(2):
+            for t in range(2):
+                share_of(r, side, t).wait_recv()
+        return [
+            dot(
+                (own[t] + from_left[r, t].astype(F32) + from_right[r, t].astype(F32)).astype(BF16),
+                order_ref[256 * r : 256 * r + 256],
+            )
+            for t in range(2)
+        ]
+
+    arrived(wall.at[o, 0], wp_recv.at[0])
     far(0)
     near(0)
     onward(0)
     weight_step(4, 1)
-    arrived(wall.at[:, :, o, 1], wp_recv.at[1])
+    arrived(wall.at[o, 1], wp_recv.at[1])
     far(1)
     near(1)
-    mine = [[project(x, t, 0) for t in range(2)]]
+    own_first = [project(x, t, 0) for t in range(2)]
     onward(1)
-    mine.append([project(x, t, 1) for t in range(2)])
+    own_second = [project(x, t, 1) for t in range(2)]
+    first = total_of(0, own_first)
+    second = total_of(1, own_second)
+    for t in range(2):
+        out_ref[:, 512 * t : 512 * t + 512] = (first[t] + second[t]).astype(BF16)
+
+    for copy in (swap_f, swap_g, swap_r, halo):
+        copy.wait_send()
+    for which, src in enumerate((send_f, send_g, send_r)):
+        arrived(src.at[pl.ds(0, CHIPS - 1)], a_send.at[which])
     for r in range(2):
-        for side in range(2):
-            share_of(r, side).wait()
-    for t in range(2):
-        pieces = [
-            (mine[r][t] + from_left[r, t].astype(F32) + from_right[r, t].astype(F32)).astype(BF16)
-            for r in range(2)
-        ]
-        out_ref[:, 512 * t : 512 * t + 512] = dot(jnp.concatenate(pieces, 1), order_ref[...]).astype(BF16)
-
-    arrived(wall.at[0, pl.ds(0, 7), s], w1_send)
-    arrived(wall.at[pl.ds(0, 7), :, s], w2_send)
-    arrived(wall.at[:, :, s], wp_send)
+        for t in range(2):
+            hop(r, t).wait_send()
+            for side in range(2):
+                share_of(r, side, t).wait_send()
+    arrived(wall.at[0, 0, 0, pl.ds(0, 7), pl.ds(0, 4)], w1_send)
+    arrived(wall.at[0, :, :, pl.ds(0, 7)], w2_send)
+    arrived(wall.at[s], wp_send)
 
 
 def local(query_act, key_act, value_act, short_filter, long_filter, out_weight):
@@ -425,12 +462,12 @@
             half_bf16, half_bf16, half_bf16, half_bf16, half_bf16, half_bf16,
             tiles, tiles, tiles, tiles, tiles, tiles,
             pltpu.VMEM((2, 4 * TOK, 2 * TOK), F32),
-            pltpu.VMEM((NY, NZ, 2, 2, 16, WIDTH), BF16),
+            pltpu.VMEM((2, 2, 2, NY, NZ, 16, WIDTH // 2), BF16),
             act,
             share_bf16, share_bf16, share_bf16, share_bf16, share_bf16, share_bf16,
             share_f32, share_f32,
-            dma((4,)), dma((4,)), dma((3,)), dma((3,)), dma, dma((2, 2)), dma, dma((2, 2, 4, 2)), dma, dma((2,)),
-            dma((2, 4)), dma((2, 4)),
+            dma((4,)), dma((4,)), dma((3,)), dma((3,)), dma, dma((2, 2, 3)), dma, dma((2, 2, 4, 2)), dma, dma((2,)),
+            dma((2, 6)), dma((2, 6)),
         ],
         compiler_params=pltpu.CompilerParams(
             collective_id=0, has_side_effects=True, vmem_limit_bytes=60 * 1024 * 1024

time: 84.2 us -> 82.4 us (0.979)
  Pallas kernels: 82.4 us -> 80.6 us
    pallas_call x1, Pallas kernels: 82.4 us -> 80.6 us  [local(): pl.pallas_call(kernel, out_shape=jax.ShapeDtypeStruct((TOK, WIDTH), BF16)...]
where the time goes in v2:
time: 82.4 us; the launch traced here: 82.3 us
  Pallas kernels  80.6 us (98%)
  local copies, waits for them, and re-layouts  1.67 us (2%)
    pallas_call x1, Pallas kernels, local(): pl.pallas_call(kernel, out_shape=jax.ShapeDtypeStruct((TOK, WIDTH), BF16)...  80.6 us
    unnamed x1, local copies, waits for them, and re-layouts  1.67 us

profile of v2, /device:TPU:1, one launch (start us, length us, event | category | flops | bytes accessed | tf_op | source)
XLA Modules:
  0.0 82.3 jit_solution(11798847146185769862)
XLA Ops:
  0.0 80.6 %shard_map.118 = bf16[128,1024]{1,0:T(8,128)(2,1)} custom-call(bf16[128,1024]{1,0:T(8,128)(2,1)} %q_hbm.1, bf16[128,1024]{1,0:T(8,128)(2,1)} %k_hbm.1, bf16[128,1024]{1,0:T(8,128)(2,1)} %v_hbm.1, f32[128,1024]{1,0:T(8,128)} %sf_hbm.1, f32[128,1024]{1,0:T(8,128)} %lf_hbm.1, bf16[32,1024]{1,0:T(8,128)(2,1)} %bitcast.1, ...), custom_call_target="tpu_custom_call" | custom-call | tf_op jit(solution)/shard_map/pallas_call | solution.py:451
  80.6 1.7 %copy.14 = bf16[128,1024]{1,0:T(8,128)(2,1)} copy(bf16[128,1024]{1,0:T(8,128)(2,1)} %shard_map.118) | data formatting | bytes 524288

commit v3 on v2

--- a/solution.py
+++ b/solution.py
@@ -175,18 +175,20 @@
             else:
                 arrived(chunk(h, 4, r, 0), w2_recv.at[h, 0, 3, r])
                 arrived(chunk(h, 4, r, 1), w2_recv.at[h, 1, 3, r])
-                share(chunk(h, 4, r), r)
             if j < 4:
                 for side in range(2):
                     moved = chunk(h, j if side else -j, r, side if j == 3 else None)
                     remote(
                         moved, moved, w2_send, w2_recv.at[h, side, j, r], toward(h, side == 0)
                     ).start()
+        for h in range(2):
             if j == 0:
                 share(chunk(h, 0, r), r)
             elif j < 4:
                 share(chunk(h, -j, r), r)
                 share(chunk(h, j, r), r)
+            else:
+                share(chunk(h, 4, r), r)
 
     loads[0].wait()
     loads[1].wait()

time: 82.4 us -> 82.4 us (level)
  no operation moved by 1% of the time
where the time goes in v3:
time: 82.4 us; the launch traced here: 82.1 us
  Pallas kernels  80.4 us (98%)
  local copies, waits for them, and re-layouts  1.67 us (2%)
    pallas_call x1, Pallas kernels, local(): pl.pallas_call(kernel, out_shape=jax.ShapeDtypeStruct((TOK, WIDTH), BF16)...  80.4 us
    unnamed x1, local copies, waits for them, and re-layouts  1.67 us

profile of v3, /device:TPU:1, one launch (start us, length us, event | category | flops | bytes accessed | tf_op | source)
XLA Modules:
  0.0 82.1 jit_solution(18325465750093964046)
XLA Ops:
  0.0 80.4 %shard_map.118 = bf16[128,1024]{1,0:T(8,128)(2,1)} custom-call(bf16[128,1024]{1,0:T(8,128)(2,1)} %q_hbm.1, bf16[128,1024]{1,0:T(8,128)(2,1)} %k_hbm.1, bf16[128,1024]{1,0:T(8,128)(2,1)} %v_hbm.1, f32[128,1024]{1,0:T(8,128)} %sf_hbm.1, f32[128,1024]{1,0:T(8,128)} %lf_hbm.1, bf16[32,1024]{1,0:T(8,128)(2,1)} %bitcast.1, ...), custom_call_target="tpu_custom_call" | custom-call | tf_op jit(solution)/shard_map/pallas_call | solution.py:453
  80.4 1.7 %copy.14 = bf16[128,1024]{1,0:T(8,128)(2,1)} copy(bf16[128,1024]{1,0:T(8,128)(2,1)} %shard_map.118) | data formatting | bytes 524288
